TPU v7x, 32 devices: a whole 2x2x4 slice. The times are simulated.
32 devices in a mesh: lat: 8 (over y, x, core), lon: 4 (over z).
Axes of the slice: x: 2, y: 2, z: 4, core: 2. Of those that a mesh axis runs over, the one named last changes fastest.
Arguments:
- grid_state: bfloat16 [120, 192, 128], P('lat', 'lon'), may hold values from -6 to 6
- weight_in: bfloat16 [6, 128, 384], replicated, may hold values from -0.5 to 0.5
- bias_in: float32 [6, 384], replicated, may hold values from -4 to 4
- weight_out: bfloat16 [6, 384, 128], replicated, may hold values from -0.3125 to 0.3125
- quad_weights: float32 [120], replicated, may hold values from 0.5 to 2
- diffusion: float32 [128], replicated, may hold values from 0.3 to 30
- legendre: bfloat16 [32, 120, 32], P('lon'), may hold values from -0.5 to 0.5
- chan_table: int32 [128], replicated, may hold values from 0 to 127, each once
- wave_table: int32 [32], replicated, may hold values from 0 to 31, each once
Outputs:
- updated: bfloat16 [120, 192, 128], P('lat', 'lon')
- spectral: float32 [32, 128, 2, 32], P('lon', 'lat')
Inputs may be any that keep to these rules, and one draw needn't show every extreme that they name: `chan_table`: each channel 0 to 127 stands exactly once. `wave_table`: each wavenumber 0 to 31 stands exactly once.
All inputs are finite; a program needn't handle non-finite values.
Results may differ from a plain program's by a relative error of at most 0.012.
Values may be sent and summed in bfloat16 or wider, within the bound.
A program may use at most 64 MiB of HBM per device.

v0:
```python
import math
import jax
import jax.numpy as jnp
from jax import lax
from jax.sharding import PartitionSpec as P


def column_layers(column_rows, weight_in, bias_in, weight_out):
    hidden_state = column_rows.astype(jnp.float32)
    for layer_idx in range(weight_in.shape[0]):
        inv_rms = lax.rsqrt(jnp.mean(hidden_state * hidden_state, axis=-1, keepdims=True) + 1e-06)
        normed = (hidden_state * inv_rms).astype(jnp.bfloat16)
        pre_act = (
            jnp.dot(normed, weight_in[layer_idx], preferred_element_type=jnp.float32)
            + bias_in[layer_idx]
        )
        activation = jax.nn.gelu(pre_act, approximate=True).astype(jnp.bfloat16)
        hidden_state = hidden_state + jnp.dot(
            activation, weight_out[layer_idx], preferred_element_type=jnp.float32
        )
    return hidden_state.astype(jnp.bfloat16)


def trig_table(wave_ids, longitudes, lon_total):
    phase_angle = (wave_ids[:, None] * longitudes[None, :] % lon_total).astype(jnp.float32) * (
        2.0 * math.pi / lon_total
    )
    stacked = jnp.stack([jnp.cos(phase_angle), -jnp.sin(phase_angle)], axis=1) / math.sqrt(
        lon_total
    )
    return stacked.astype(jnp.bfloat16)


def pick_channels(rows, chosen):
    picked = jnp.einsum("ljc,ck->ljk", rows, chosen, preferred_element_type=jnp.float32)
    return picked.astype(jnp.bfloat16)


def local(
    grid_state,
    weight_in,
    bias_in,
    weight_out,
    quad_weights,
    diffusion,
    legendre,
    chan_table,
    wave_table,
):
    lat_rows, lon_cols, channels = grid_state.shape
    lat_count = lax.axis_size("lat")
    lon_count = lax.axis_size("lon")
    lon_total = lon_cols * lon_count
    per_dev = channels // lat_count
    owned_slots = legendre.shape[0]
    top_degree = legendre.shape[2]
    flat_rows = grid_state.reshape(lat_rows * lon_cols, channels)
    columns = column_layers(flat_rows, weight_in, bias_in, weight_out).reshape(
        lat_rows, lon_cols, channels
    )
    every = jnp.arange(channels, dtype=jnp.int32)
    chosen = (every[:, None] == chan_table[None, :]).astype(jnp.bfloat16)
    ordered = pick_channels(columns, chosen)
    levels = lax.all_to_all(ordered, "lat", split_axis=2, concat_axis=0, tiled=True)
    trig_all = trig_table(wave_table, jnp.arange(lon_total, dtype=jnp.int32), lon_total)
    lon_here = lax.axis_index("lon") * lon_cols + jnp.arange(lon_cols, dtype=jnp.int32)
    trig_rows = trig_table(wave_table, lon_here, lon_total)
    fourier = lax.psum_scatter(
        jnp.einsum("srj,ljk->skrl", trig_rows, levels, preferred_element_type=jnp.float32),
        "lon",
        scatter_dimension=0,
        tiled=True,
    )
    weighted = (fourier * quad_weights).astype(jnp.bfloat16)
    raw_spec = jnp.einsum("skrl,sln->skrn", weighted, legendre, preferred_element_type=jnp.float32)
    my_waves = lax.dynamic_slice_in_dim(
        wave_table, lax.axis_index("lon") * owned_slots, owned_slots, 0
    )
    degree = jnp.arange(top_degree, dtype=jnp.int32)
    triangle = (degree[None, :] >= my_waves[:, None]).astype(jnp.float32)
    my_chans = lax.dynamic_slice_in_dim(chan_table, lax.axis_index("lat") * per_dev, per_dev, 0)
    degree_f = degree.astype(jnp.float32)
    damping = (
        jnp.sum(jnp.where(my_chans[:, None] == every[None, :], diffusion[None, :], 0.0), 1)[:, None]
        * (degree_f * (degree_f + 1.0))[None, :]
        / float(top_degree * top_degree)
    )
    spectral = raw_spec * triangle[:, None, None, :] / (1.0 + damping)[None, :, None, :]
    back_fourier = jnp.einsum(
        "skrn,sln->skrl",
        spectral.astype(jnp.bfloat16),
        legendre,
        preferred_element_type=jnp.float32,
    ).astype(jnp.bfloat16)
    all_waves = lax.all_to_all(back_fourier, "lon", split_axis=3, concat_axis=0, tiled=True)
    band_tendency = jnp.einsum(
        "skrl,srj->ljk", all_waves, trig_all, preferred_element_type=jnp.float32
    ).astype(jnp.bfloat16)
    tendency = lax.all_to_all(
        lax.all_to_all(band_tendency, "lon", split_axis=1, concat_axis=0, tiled=True),
        "lat",
        split_axis=0,
        concat_axis=2,
        tiled=True,
    )
    tendency = pick_channels(tendency, chosen.T)
    updated = (columns.astype(jnp.float32) + tendency.astype(jnp.float32)).astype(jnp.bfloat16)
    return (updated, spectral)


def solution(mesh):
    placed = (P("lat", "lon", None), P(), P(), P(), P(), P(), P("lon", None, None), P(), P())
    return jax.shard_map(
        local,
        mesh=mesh,
        in_specs=placed,
        out_specs=(P("lat", "lon", None), P("lon", "lat", None, None)),
        check_vma=False,
    )
```

profile of v0, /device:TPU:0, one launch (start us, length us, event | category | flops | bytes accessed | tf_op | source)
XLA Modules:
  0.0 100.8 jit_solution(6014327949595269104)
XLA Ops:
  7.2 1.1 %multiply_reduce_fusion.5 = f32[15,48]{1,0:T(8,128)S(1)} fusion(bf16[15,48,128]{2,1,0:T(8,128)(2,1)} %param.9), kind=kLoop, calls=%fused_computation.121 | loop fusion | flops 275760 | bytes 187200 | tf_op jit(solution)/shard_map/reduce_sum | solution.py:11
  8.3 1.0 slice_reduce_fusion
  9.3 1.1 %multiply_convert_fusion.15 = bf16[15,48,128]{2,1,0:T(8,128)(2,1)S(1)} fusion(bf16[15,48,128]{2,1,0:T(8,128)(2,1)} %param.9, f32[15,48]{1,0:T(8,128)S(1)} %add_rsqrt_fusion), kind=kLoop, calls=%fused_computation.120 | loop fusion | flops 276480 | bytes 371520 | tf_op jit(solution)/shard_map/convert_element_type | solution.py:12
  10.4 1.9 %multiply_reduce_fusion.4 = (f32[720]{0:T(1024)S(1)}, f32[720,128]{1,0:T(8,128)S(1)}) fusion(bf16[6,384,128]{2,1,0:T(8,128)(2,1)} %param.12, bf16[720,128]{1,0:T(8,128)(2,1)S(1)} %bitcast.139, f32[384]{0:T(512)S(1)} %get-tuple-element.14, bf16[6,128,384]{2,1,0:T(8,128)(2,1)} %param.10, bf16[720,128]{1,0:T(8,128)(2,1)} %bitcast.136), kind=kOutput, calls=%fused_computation.119 | convolution fusion | flops 144690480 | bytes 938304 | tf_op jit(solution)/shard_map/dot_general | solution.py:18
  13.2 0.9 multiply_reduce_fusion.2
  14.1 0.9 multiply_reduce_fusion.1
  15.0 0.9 multiply_reduce_fusion
  17.4 1.4 %reshape.324 = bf16[8,2,5760]{2,1,0:T(2,128)(2,1)} reshape(bf16[128,15,48]{2,1,0:T(8,128)(2,1)S(1)} %bitcast.127) | data formatting | bytes 368640
  18.8 5.2 %all-to-all-start = ((bf16[8,2,5760]{2,1,0:T(2,128)(2,1)}), bf16[8,2,5760]{2,1,0:T(2,128)(2,1)S(1)}, u32[]{:S(2)}, u32[]{:S(2)}) async-start(bf16[8,2,5760]{2,1,0:T(2,128)(2,1)} %reshape.324), calls=%async_computation | async-start | bytes 368640 | tf_op jit(solution)/shard_map/all_to_all | solution.py:64
  24.2 5.9 %all-to-all-done = bf16[8,2,5760]{2,1,0:T(2,128)(2,1)S(1)} async-done(((bf16[8,2,5760]{2,1,0:T(2,128)(2,1)}), bf16[8,2,5760]{2,1,0:T(2,128)(2,1)S(1)}, u32[]{:S(2)}, u32[]{:S(2)}) %all-to-all-start) | async-done | bytes 184352 | tf_op jit(solution)/shard_map/all_to_all | solution.py:64
  30.8 1.2 %convolution_bitcast_fusion.1 = f32[32,16,2,120]{3,0,2,1:T(8,128)} fusion(bf16[120,48,16,1]{1,2,0,3:T(8,128)(2,1)S(1)} %bitcast.129, f32[32,1,48]{2,0,1:T(8,128)S(1)} %get-tuple-element.17, f32[32,1,48]{2,0,1:T(8,128)S(1)} %get-tuple-element.16), kind=kOutput, calls=%fused_computation.13 | convolution fusion | flops 11805696 | bytes 688128 | tf_op jit(solution)/shard_map/srj,ljk->skrl/dot_general | solution.py:69
  32.6 20.7 %reduce-scatter.2.cloned.1.call-done = f32[8,16,2,120]{3,0,2,1:T(8,128)} async-done(((f32[32,16,2,120]{3,0,2,1:T(8,128)}), f32[8,16,2,120]{3,0,2,1:T(8,128)}) %reduce-scatter.2.cloned.1.call-update) | async-done | bytes 122896 | tf_op jit(solution)/shard_map/reduce_scatter | solution.py:68
  53.3 0.9 multiply_convert_fusion.16
  55.0 1.0 %reshape.326 = bf16[4,2,3840]{2,1,0:T(2,128)(2,1)} reshape(bf16[120,8,2,16]{3,2,1,0:T(2,128)(2,1)S(1)} %bitcast.131) | data formatting | bytes 122880
  56.0 3.3 %all-to-all-start.1 = ((bf16[4,2,3840]{2,1,0:T(2,128)(2,1)}), bf16[4,2,3840]{2,1,0:T(2,128)(2,1)S(1)}, u32[]{:S(2)}, u32[]{:S(2)}) async-start(bf16[4,2,3840]{2,1,0:T(2,128)(2,1)} %reshape.326), calls=%async_computation.2 | async-start | bytes 122880 | tf_op jit(solution)/shard_map/all_to_all | solution.py:95
  59.5 5.5 %all-to-all-done.1 = bf16[4,2,3840]{2,1,0:T(2,128)(2,1)S(1)} async-done(((bf16[4,2,3840]{2,1,0:T(2,128)(2,1)}), bf16[4,2,3840]{2,1,0:T(2,128)(2,1)S(1)}, u32[]{:S(2)}, u32[]{:S(2)}) %all-to-all-start.1) | async-done | bytes 61472 | tf_op jit(solution)/shard_map/all_to_all | solution.py:95
  67.2 1.4 %reshape.328 = bf16[4,2,11520]{2,1,0:T(2,128)(2,1)S(1)} reshape(bf16[192,16,30]{2,1,0:T(8,128)(2,1)S(1)} %bitcast.126) | data formatting | bytes 368640
  68.7 9.1 %all_to_all.72 = bf16[4,2,11520]{2,1,0:T(2,128)(2,1)S(1)} all-to-all(bf16[4,2,11520]{2,1,0:T(2,128)(2,1)S(1)} %reshape.328), channel_id=1, replica_groups=mesh['lat'=8,'lon'=4] {'lon'}, dimensions={0} | all-to-all | bytes 368640 | tf_op jit(solution)/shard_map/all_to_all | solution.py:100
  77.8 2.1 %reshape.329 = bf16[192,16,30]{2,1,0:T(8,128)(2,1)S(1)} reshape(bf16[4,2,11520]{2,1,0:T(2,128)(2,1)S(1)} %all_to_all.72) | data formatting | bytes 368640
  79.9 1.3 %copy.57 = bf16[30,4,48,16]{2,1,3,0:T(4,128)(2,1)S(1)} copy(bf16[30,4,48,16]{0,3,2,1:T(8,128)(2,1)S(1)} %bitcast.125) | data formatting | bytes 368640 | tf_op jit(solution)/shard_map/all_to_all | solution.py:100
  81.3 1.4 %reshape.330 = bf16[8,2,5760]{2,1,0:T(2,128)(2,1)} reshape(bf16[120,16,48]{2,1,0:T(8,128)(2,1)S(1)} %bitcast.134) | data formatting | bytes 368640
  82.7 3.6 %all-to-all-start.3 = ((bf16[8,2,5760]{2,1,0:T(2,128)(2,1)}), bf16[8,2,5760]{2,1,0:T(2,128)(2,1)S(1)}, u32[]{:S(2)}, u32[]{:S(2)}) async-start(bf16[8,2,5760]{2,1,0:T(2,128)(2,1)} %reshape.330), calls=%async_computation.4 | async-start | bytes 368640 | tf_op jit(solution)/shard_map/all_to_all | solution.py:99
  87.0 5.4 %all-to-all-done.3 = bf16[8,2,5760]{2,1,0:T(2,128)(2,1)S(1)} async-done(((bf16[8,2,5760]{2,1,0:T(2,128)(2,1)}), bf16[8,2,5760]{2,1,0:T(2,128)(2,1)S(1)}, u32[]{:S(2)}, u32[]{:S(2)}) %all-to-all-start.3) | async-done | bytes 184352 | tf_op jit(solution)/shard_map/all_to_all | solution.py:99
  92.9 1.0 fusion.3
  (48 shorter events, 8.4 us)
Async XLA Ops:
  7.2 47.0 %copy-start = (bf16[8,120,32]{1,2,0:T(8,128)(2,1)S(1)}, bf16[8,120,32]{1,2,0:T(8,128)(2,1)}, u32[]{:S(2)}) copy-start(bf16[8,120,32]{1,2,0:T(8,128)(2,1)} %param.15) | copy-start | bytes 184324
  10.4 1.9 %copy-start.4 = (bf16[6,384,128]{2,1,0:T(8,128)(2,1)S(1)}, bf16[6,384,128]{2,1,0:T(8,128)(2,1)}, u32[]{:S(2)}) copy-start(bf16[6,384,128]{2,1,0:T(8,128)(2,1)} %param.12) | copy-start | bytes 1769476
  10.4 1.9 %copy-start.5 = (bf16[6,128,384]{2,1,0:T(8,128)(2,1)S(1)}, bf16[6,128,384]{2,1,0:T(8,128)(2,1)}, u32[]{:S(2)}) copy-start(bf16[6,128,384]{2,1,0:T(8,128)(2,1)} %param.10) | copy-start | bytes 1769476
  15.9 0.8 copy-start.2
  17.0 7.1 %copy-start.1 = (s32[32]{0:T(128)S(1)}, s32[32]{0:T(128)}, u32[]{:S(2)}) copy-start(s32[32]{0:T(128)} %param.17) | copy-start | bytes 388
  18.8 11.3 %all-to-all-start = ((bf16[8,2,5760]{2,1,0:T(2,128)(2,1)}), bf16[8,2,5760]{2,1,0:T(2,128)(2,1)S(1)}, u32[]{:S(2)}, u32[]{:S(2)}) async-start(bf16[8,2,5760]{2,1,0:T(2,128)(2,1)} %reshape.324), calls=%async_computation | async-start | bytes 368640 | tf_op jit(solution)/shard_map/all_to_all | solution.py:64
  24.0 29.3 %reduce-scatter.2.cloned.1.call-start = ((), (), s32[]{:S(2)}) async-start(), calls=%async_computation.5 | async-start | bytes 655360 | tf_op jit(solution)/shard_map/reduce_scatter | solution.py:68
  30.8 1.4 %copy-start.6 = (f32[128]{0:T(128)S(1)}, f32[128]{0:T(128)}, u32[]{:S(2)}) copy-start(f32[128]{0:T(128)} %param.14) | copy-start | bytes 1540
  30.8 22.4 %copy-start.3 = (f32[120]{0:T(128)S(1)}, f32[120]{0:T(128)}, u32[]{:S(2)}) copy-start(f32[120]{0:T(128)} %param.13) | copy-start | bytes 1444
  56.0 9.0 %all-to-all-start.1 = ((bf16[4,2,3840]{2,1,0:T(2,128)(2,1)}), bf16[4,2,3840]{2,1,0:T(2,128)(2,1)S(1)}, u32[]{:S(2)}, u32[]{:S(2)}) async-start(bf16[4,2,3840]{2,1,0:T(2,128)(2,1)} %reshape.326), calls=%async_computation.2 | async-start | bytes 122880 | tf_op jit(solution)/shard_map/all_to_all | solution.py:95
  82.7 9.7 %all-to-all-start.3 = ((bf16[8,2,5760]{2,1,0:T(2,128)(2,1)}), bf16[8,2,5760]{2,1,0:T(2,128)(2,1)S(1)}, u32[]{:S(2)}, u32[]{:S(2)}) async-start(bf16[8,2,5760]{2,1,0:T(2,128)(2,1)} %reshape.330), calls=%async_computation.4 | async-start | bytes 368640 | tf_op jit(solution)/shard_map/all_to_all | solution.py:99
Sparse Core Ops, SparseCore 0:
  32.2 20.9 reduce-scatter.1
where the time goes:
time: 101 us
  waiting for transfers between devices  37.4 us (37%)
  local copies, waits for them, and re-layouts  14.7 us (15%)
  between operations  14.3 us (14%)
  starting transfers between devices  12.1 us (12%)
  matrix products  9.23 us (9%)
  blocking collectives  9.13 us (9%)
  other arithmetic  3.88 us (4%)
    reduce_scatter x1, waiting for transfers between devices, local(): lax.psum_scatter(jnp.einsum('srj,ljk->skrl', trig_rows, levels, preferred...  20.7 us
    unnamed x23, local copies, waits for them, and re-layouts  9.62 us
    all_to_all x1, blocking collectives, local(): lax.all_to_all(band_tendency, 'lon', split_axis=1, concat_axis=0, tiled=T...  9.13 us
    dot_general x6, matrix products, column_layers(): jnp.dot(activation, weight_out[layer_idx], preferred_element_type=jnp.flo...  6.23 us
    all_to_all x1, waiting for transfers between devices, local(): lax.all_to_all(ordered, 'lat', split_axis=2, concat_axis=0, tiled=True)  5.87 us
    all_to_all x1, waiting for transfers between devices, local(): lax.all_to_all(back_fourier, 'lon', split_axis=3, concat_axis=0, tiled=True)  5.47 us
    all_to_all x1, waiting for transfers between devices, local(): lax.all_to_all(lax.all_to_all(band_tendency, 'lon', split_axis=1, concat_...  5.38 us
    all_to_all x1, starting transfers between devices, local(): lax.all_to_all(ordered, 'lat', split_axis=2, concat_axis=0, tiled=True)  5.18 us
  transfers between devices with their start and end apart: 4, of which 4 were waited for; matrix products, arithmetic and copies ran while one was open for 2% of the time, Pallas kernels for 0%

commit v1 on v0

--- a/solution.py
+++ b/solution.py
@@ -3,6 +3,22 @@
 import jax.numpy as jnp
 from jax import lax
 from jax.sharding import PartitionSpec as P
+
+
+def swapped_with_each(array, axis, split, join):
+    ways, here = (lax.axis_size(axis), lax.axis_index(axis))
+    width = array.shape[split] // ways
+    shape = list(array.shape)
+    shape[split] = width
+    height = shape[join]
+    shape[join] = height * ways
+    full = jnp.zeros(shape, array.dtype)
+    for mask in range(ways):
+        part = lax.dynamic_slice_in_dim(array, (here ^ mask) * width, width, axis=split)
+        if mask:
+            part = lax.ppermute(part, axis, [(d, d ^ mask) for d in range(ways)])
+        full = lax.dynamic_update_slice_in_dim(full, part, (here ^ mask) * height, axis=join)
+    return full
 
 
 def column_layers(column_rows, weight_in, bias_in, weight_out):
@@ -97,7 +113,7 @@
         "skrl,srj->ljk", all_waves, trig_all, preferred_element_type=jnp.float32
     ).astype(jnp.bfloat16)
     tendency = lax.all_to_all(
-        lax.all_to_all(band_tendency, "lon", split_axis=1, concat_axis=0, tiled=True),
+        swapped_with_each(band_tendency, "lon", 1, 0),
         "lat",
         split_axis=0,
         concat_axis=2,

time: 101 us -> 98 us (0.970)
  blocking collectives: 9.13 us -> 0 us
  waiting for transfers between devices: 37.4 us -> 43.9 us
  local copies, waits for them, and re-layouts: 14.7 us -> 9.73 us
  starting transfers between devices: 12.1 us -> 16.3 us
    all_to_all x1 -> x0, blocking collectives: 9.13 us -> none  [local(): lax.all_to_all(band_tendency, 'lon', split_axis=1, concat_axis=0, tiled=T...]
    ppermute x0 -> x3, waiting for transfers between devices: none -> 6.63 us  [swapped_with_each(): part = lax.ppermute(part, axis, [(d, d ^ mask) for d in range(ways)])]
    ppermute x0 -> x3, starting transfers between devices: none -> 4.45 us  [swapped_with_each(): part = lax.ppermute(part, axis, [(d, d ^ mask) for d in range(ways)])]
    unnamed x23, local copies, waits for them, and re-layouts: 9.62 us -> 6.07 us
    all_to_all x3 -> x1, local copies, waits for them, and re-layouts: 1.42 us -> 0.04 us  [local(): lax.all_to_all(swapped_with_each(band_tendency, 'lon', 1, 0), 'lat', spli...]
  transfers between devices with their start and end apart: 4 -> 7, of which waited for: 4 -> 6; matrix products, arithmetic and copies ran while one was open for 2% -> 2% of each run, Pallas kernels for 0% -> 0%
where the time goes in v1:
time: 98 us; the launch traced here: 97.4 us
  waiting for transfers between devices  43.9 us (45%)
  starting transfers between devices  16.3 us (17%)
  between operations  14.4 us (15%)
  local copies, waits for them, and re-layouts  9.73 us (10%)
  matrix products  9.16 us (9%)
  other arithmetic  3.92 us (4%)
    reduce_scatter x1, waiting for transfers between devices, local(): lax.psum_scatter(jnp.einsum('srj,ljk->skrl', trig_rows, levels, preferred...  20.7 us
    ppermute x3, waiting for transfers between devices, swapped_with_each(): part = lax.ppermute(part, axis, [(d, d ^ mask) for d in range(ways)])  6.63 us
    dot_general x6, matrix products, column_layers(): jnp.dot(activation, weight_out[layer_idx], preferred_element_type=jnp.flo...  6.15 us
    unnamed x23, local copies, waits for them, and re-layouts  6.07 us
    all_to_all x1, waiting for transfers between devices, local(): lax.all_to_all(ordered, 'lat', split_axis=2, concat_axis=0, tiled=True)  5.87 us
    all_to_all x1, waiting for transfers between devices, local(): lax.all_to_all(back_fourier, 'lon', split_axis=3, concat_axis=0, tiled=True)  5.44 us
    all_to_all x1, waiting for transfers between devices, local(): lax.all_to_all(swapped_with_each(band_tendency, 'lon', 1, 0), 'lat', spli...  5.31 us
    all_to_all x1, starting transfers between devices, local(): lax.all_to_all(ordered, 'lat', split_axis=2, concat_axis=0, tiled=True)  5.18 us
  transfers between devices with their start and end apart: 7, of which 6 were waited for; matrix products, arithmetic and copies ran while one was open for 2% of the time, Pallas kernels for 0%

profile of v1, /device:TPU:0, one launch (start us, length us, event | category | flops | bytes accessed | tf_op | source)
XLA Modules:
  0.0 97.4 jit_solution(12486780858339281129)
XLA Ops:
  7.2 1.2 %multiply_reduce_fusion.5 = f32[15,48]{1,0:T(8,128)S(1)} fusion(bf16[15,48,128]{2,1,0:T(8,128)(2,1)} %param.9), kind=kLoop, calls=%fused_computation.120 | loop fusion | flops 275760 | bytes 187200 | tf_op jit(solution)/shard_map/reduce_sum | solution.py:27
  8.4 1.0 slice_reduce_fusion
  9.3 1.1 %multiply_convert_fusion.15 = bf16[15,48,128]{2,1,0:T(8,128)(2,1)S(1)} fusion(bf16[15,48,128]{2,1,0:T(8,128)(2,1)} %param.9, f32[15,48]{1,0:T(8,128)S(1)} %add_rsqrt_fusion), kind=kLoop, calls=%fused_computation.119 | loop fusion | flops 276480 | bytes 371520 | tf_op jit(solution)/shard_map/convert_element_type | solution.py:28
  10.4 1.8 %multiply_reduce_fusion.4 = (f32[720]{0:T(1024)S(1)}, f32[720,128]{1,0:T(8,128)S(1)}) fusion(bf16[6,384,128]{2,1,0:T(8,128)(2,1)} %param.12, bf16[720,128]{1,0:T(8,128)(2,1)S(1)} %bitcast.135, f32[384]{0:T(512)S(1)} %get-tuple-element.14, bf16[6,128,384]{2,1,0:T(8,128)(2,1)} %param.10, bf16[720,128]{1,0:T(8,128)(2,1)S(1)} %bitcast.132), kind=kOutput, calls=%fused_computation.118 | convolution fusion | flops 144690480 | bytes 938304 | tf_op jit(solution)/shard_map/dot_general | solution.py:34
  12.3 0.9 multiply_reduce_fusion.3
  13.2 0.9 multiply_reduce_fusion.2
  14.1 0.9 multiply_reduce_fusion.1
  17.4 1.4 %reshape.324 = bf16[8,2,5760]{2,1,0:T(2,128)(2,1)} reshape(bf16[128,15,48]{2,1,0:T(8,128)(2,1)S(1)} %bitcast.124) | data formatting | bytes 368640
  18.8 5.2 %all-to-all-start = ((bf16[8,2,5760]{2,1,0:T(2,128)(2,1)}), bf16[8,2,5760]{2,1,0:T(2,128)(2,1)S(1)}, u32[]{:S(2)}, u32[]{:S(2)}) async-start(bf16[8,2,5760]{2,1,0:T(2,128)(2,1)} %reshape.324), calls=%async_computation | async-start | bytes 368640 | tf_op jit(solution)/shard_map/all_to_all | solution.py:80
  24.2 5.9 %all-to-all-done = bf16[8,2,5760]{2,1,0:T(2,128)(2,1)S(1)} async-done(((bf16[8,2,5760]{2,1,0:T(2,128)(2,1)}), bf16[8,2,5760]{2,1,0:T(2,128)(2,1)S(1)}, u32[]{:S(2)}, u32[]{:S(2)}) %all-to-all-start) | async-done | bytes 184352 | tf_op jit(solution)/shard_map/all_to_all | solution.py:80
  30.8 1.2 %convolution_bitcast_fusion.1 = f32[32,16,2,120]{3,0,2,1:T(8,128)} fusion(bf16[120,48,16,1]{1,2,0,3:T(8,128)(2,1)S(1)} %bitcast.126, f32[32,1,48]{2,0,1:T(8,128)S(1)} %get-tuple-element.21, f32[32,1,48]{2,0,1:T(8,128)S(1)} %get-tuple-element.20), kind=kOutput, calls=%fused_computation.13 | convolution fusion | flops 11805696 | bytes 688128 | tf_op jit(solution)/shard_map/srj,ljk->skrl/dot_general | solution.py:85
  32.6 20.7 %reduce-scatter.2.cloned.1.call-done = f32[8,16,2,120]{3,0,2,1:T(8,128)} async-done(((f32[32,16,2,120]{3,0,2,1:T(8,128)}), f32[8,16,2,120]{3,0,2,1:T(8,128)}) %reduce-scatter.2.cloned.1.call-update) | async-done | bytes 122896 | tf_op jit(solution)/shard_map/reduce_scatter | solution.py:84
  53.2 0.9 multiply_convert_fusion.16
  54.9 1.0 %reshape.326 = bf16[4,2,3840]{2,1,0:T(2,128)(2,1)} reshape(bf16[120,8,2,16]{3,2,1,0:T(2,128)(2,1)S(1)} %bitcast.129) | data formatting | bytes 122880
  56.0 3.3 %all-to-all-start.1 = ((bf16[4,2,3840]{2,1,0:T(2,128)(2,1)}), bf16[4,2,3840]{2,1,0:T(2,128)(2,1)S(1)}, u32[]{:S(2)}, u32[]{:S(2)}) async-start(bf16[4,2,3840]{2,1,0:T(2,128)(2,1)} %reshape.326), calls=%async_computation.2 | async-start | bytes 122880 | tf_op jit(solution)/shard_map/all_to_all | solution.py:111
  59.5 5.4 %all-to-all-done.1 = bf16[4,2,3840]{2,1,0:T(2,128)(2,1)S(1)} async-done(((bf16[4,2,3840]{2,1,0:T(2,128)(2,1)}), bf16[4,2,3840]{2,1,0:T(2,128)(2,1)S(1)}, u32[]{:S(2)}, u32[]{:S(2)}) %all-to-all-start.1) | async-done | bytes 61472 | tf_op jit(solution)/shard_map/all_to_all | solution.py:111
  67.6 1.6 %collective-permute-start.1 = (bf16[30,48,16]{1,0,2:T(8,128)(2,1)S(1)}, bf16[30,48,16]{1,0,2:T(8,128)(2,1)S(1)}, u32[]{:S(2)}, u32[]{:S(2)}) collective-permute-start(bf16[30,48,16]{1,0,2:T(8,128)(2,1)S(1)} %get-tuple-element.17), channel_id=1, source_target_pairs={{0,2},{1,3},{2,0},{3,1},{4,6},{5,7},{6,4},{7,5},{8,10},{9,11},{10,... | collective-permute-start | bytes 138248 | tf_op jit(solution)/shard_map/ppermute | solution.py:19
  69.2 2.0 %collective-permute-start = (bf16[30,48,16]{1,0,2:T(8,128)(2,1)S(1)}, bf16[30,48,16]{1,0,2:T(8,128)(2,1)S(1)}, u32[]{:S(2)}, u32[]{:S(2)}) collective-permute-start(bf16[30,48,16]{1,0,2:T(8,128)(2,1)S(1)} %get-tuple-element.18), channel_id=1, source_target_pairs={{0,1},{1,0},{2,3},{3,2},{4,5},{5,4},{6,7},{7,6},{8,9},{9,8},{10,11... | collective-permute-start | bytes 138248 | tf_op jit(solution)/shard_map/ppermute | solution.py:19
  71.4 4.0 %collective-permute-done = bf16[30,48,16]{1,0,2:T(8,128)(2,1)S(1)} collective-permute-done((bf16[30,48,16]{1,0,2:T(8,128)(2,1)S(1)}, bf16[30,48,16]{1,0,2:T(8,128)(2,1)S(1)}, u32[]{:S(2)}, u32[]{:S(2)}) %collective-permute-start) | collective-permute-done | bytes 46112 | tf_op jit(solution)/shard_map/ppermute | solution.py:19
  75.5 2.6 %collective-permute-done.1 = bf16[30,48,16]{1,0,2:T(8,128)(2,1)S(1)} collective-permute-done((bf16[30,48,16]{1,0,2:T(8,128)(2,1)S(1)}, bf16[30,48,16]{1,0,2:T(8,128)(2,1)S(1)}, u32[]{:S(2)}, u32[]{:S(2)}) %collective-permute-start.1) | collective-permute-done | bytes 46112 | tf_op jit(solution)/shard_map/ppermute | solution.py:19
  78.2 1.4 %reshape.328 = bf16[8,2,5760]{2,1,0:T(2,128)(2,1)} reshape(bf16[120,16,48]{2,1,0:T(8,128)(2,1)S(1)} %bitcast.127) | data formatting | bytes 368640
  79.6 3.4 %all-to-all-start.2 = ((bf16[8,2,5760]{2,1,0:T(2,128)(2,1)}), bf16[8,2,5760]{2,1,0:T(2,128)(2,1)S(1)}, u32[]{:S(2)}, u32[]{:S(2)}) async-start(bf16[8,2,5760]{2,1,0:T(2,128)(2,1)} %reshape.328), calls=%async_computation.3 | async-start | bytes 368640 | tf_op jit(solution)/shard_map/all_to_all | solution.py:115
  83.7 5.3 %all-to-all-done.2 = bf16[8,2,5760]{2,1,0:T(2,128)(2,1)S(1)} async-done(((bf16[8,2,5760]{2,1,0:T(2,128)(2,1)}), bf16[8,2,5760]{2,1,0:T(2,128)(2,1)S(1)}, u32[]{:S(2)}, u32[]{:S(2)}) %all-to-all-start.2) | async-done | bytes 184352 | tf_op jit(solution)/shard_map/all_to_all | solution.py:115
  89.6 1.0 %fusion.3 = bf16[15,48,128]{2,1,0:T(8,128)(2,1)} fusion(bf16[15,48,128]{1,2,0:T(8,128)(2,1)S(1)} %bitcast.128, bf16[15,48,128]{2,1,0:T(8,128)(2,1)S(1)} %bitcast.134, s32[128]{0:T(128)S(1)} %copy-done.3), kind=kOutput, calls=%fused_computation.25 | convolution fusion | flops 24070144 | bytes 553472 | tf_op jit(solution)/shard_map/ljc,ck->ljk/dot_general | solution.py:51
  (56 shorter events, 9.1 us)
Async XLA Ops:
  7.2 47.0 %copy-start = (bf16[8,120,32]{1,2,0:T(8,128)(2,1)S(1)}, bf16[8,120,32]{1,2,0:T(8,128)(2,1)}, u32[]{:S(2)}) copy-start(bf16[8,120,32]{1,2,0:T(8,128)(2,1)} %param.15) | copy-start | bytes 184324
  7.2 3.2 %copy-start.1 = (bf16[15,48,128]{2,1,0:T(8,128)(2,1)S(1)}, bf16[15,48,128]{2,1,0:T(8,128)(2,1)}, u32[]{:S(2)}) copy-start(bf16[15,48,128]{2,1,0:T(8,128)(2,1)} %param.9) | copy-start | bytes 552964
  10.4 1.9 %copy-start.5 = (bf16[6,384,128]{2,1,0:T(8,128)(2,1)S(1)}, bf16[6,384,128]{2,1,0:T(8,128)(2,1)}, u32[]{:S(2)}) copy-start(bf16[6,384,128]{2,1,0:T(8,128)(2,1)} %param.12) | copy-start | bytes 1769476
  10.4 1.9 %copy-start.6 = (bf16[6,128,384]{2,1,0:T(8,128)(2,1)S(1)}, bf16[6,128,384]{2,1,0:T(8,128)(2,1)}, u32[]{:S(2)}) copy-start(bf16[6,128,384]{2,1,0:T(8,128)(2,1)} %param.10) | copy-start | bytes 1769476
  15.9 0.8 copy-start.3
  17.4 6.6 %copy-start.2 = (s32[32]{0:T(128)S(1)}, s32[32]{0:T(128)}, u32[]{:S(2)}) copy-start(s32[32]{0:T(128)} %param.17) | copy-start | bytes 388
  18.8 11.3 %all-to-all-start = ((bf16[8,2,5760]{2,1,0:T(2,128)(2,1)}), bf16[8,2,5760]{2,1,0:T(2,128)(2,1)S(1)}, u32[]{:S(2)}, u32[]{:S(2)}) async-start(bf16[8,2,5760]{2,1,0:T(2,128)(2,1)} %reshape.324), calls=%async_computation | async-start | bytes 368640 | tf_op jit(solution)/shard_map/all_to_all | solution.py:80
  23.9 29.3 %reduce-scatter.2.cloned.1.call-start = ((), (), s32[]{:S(2)}) async-start(), calls=%async_computation.4 | async-start | bytes 655360 | tf_op jit(solution)/shard_map/reduce_scatter | solution.py:84
  30.8 1.4 %copy-start.7 = (f32[128]{0:T(128)S(1)}, f32[128]{0:T(128)}, u32[]{:S(2)}) copy-start(f32[128]{0:T(128)} %param.14) | copy-start | bytes 1540
  30.8 22.4 %copy-start.4 = (f32[120]{0:T(128)S(1)}, f32[120]{0:T(128)}, u32[]{:S(2)}) copy-start(f32[120]{0:T(128)} %param.13) | copy-start | bytes 1444
  56.0 9.0 %all-to-all-start.1 = ((bf16[4,2,3840]{2,1,0:T(2,128)(2,1)}), bf16[4,2,3840]{2,1,0:T(2,128)(2,1)S(1)}, u32[]{:S(2)}, u32[]{:S(2)}) async-start(bf16[4,2,3840]{2,1,0:T(2,128)(2,1)} %reshape.326), calls=%async_computation.2 | async-start | bytes 122880 | tf_op jit(solution)/shard_map/all_to_all | solution.py:111
  66.8 11.4 %collective-permute-start.2 = (bf16[30,48,16]{1,0,2:T(8,128)(2,1)S(1)}, bf16[30,48,16]{1,0,2:T(8,128)(2,1)S(1)}, u32[]{:S(2)}, u32[]{:S(2)}) collective-permute-start(bf16[30,48,16]{1,0,2:T(8,128)(2,1)S(1)} %get-tuple-element.16), channel_id=1, source_target_pairs={{0,3},{1,2},{2,1},{3,0},{4,7},{5,6},{6,5},{7,4},{8,11},{9,10},{10,... | collective-permute-start | bytes 138248 | tf_op jit(solution)/shard_map/ppermute | solution.py:19
  67.6 10.5 %collective-permute-start.1 = (bf16[30,48,16]{1,0,2:T(8,128)(2,1)S(1)}, bf16[30,48,16]{1,0,2:T(8,128)(2,1)S(1)}, u32[]{:S(2)}, u32[]{:S(2)}) collective-permute-start(bf16[30,48,16]{1,0,2:T(8,128)(2,1)S(1)} %get-tuple-element.17), channel_id=1, source_target_pairs={{0,2},{1,3},{2,0},{3,1},{4,6},{5,7},{6,4},{7,5},{8,10},{9,11},{10,... | collective-permute-start | bytes 138248 | tf_op jit(solution)/shard_map/ppermute | solution.py:19
  69.2 6.2 %collective-permute-start = (bf16[30,48,16]{1,0,2:T(8,128)(2,1)S(1)}, bf16[30,48,16]{1,0,2:T(8,128)(2,1)S(1)}, u32[]{:S(2)}, u32[]{:S(2)}) collective-permute-start(bf16[30,48,16]{1,0,2:T(8,128)(2,1)S(1)} %get-tuple-element.18), channel_id=1, source_target_pairs={{0,1},{1,0},{2,3},{3,2},{4,5},{5,4},{6,7},{7,6},{8,9},{9,8},{10,11... | collective-permute-start | bytes 138248 | tf_op jit(solution)/shard_map/ppermute | solution.py:19
  79.6 9.4 %all-to-all-start.2 = ((bf16[8,2,5760]{2,1,0:T(2,128)(2,1)}), bf16[8,2,5760]{2,1,0:T(2,128)(2,1)S(1)}, u32[]{:S(2)}, u32[]{:S(2)}) async-start(bf16[8,2,5760]{2,1,0:T(2,128)(2,1)} %reshape.328), calls=%async_computation.3 | async-start | bytes 368640 | tf_op jit(solution)/shard_map/all_to_all | solution.py:115
Sparse Core Ops, SparseCore 0:
  32.2 20.9 reduce-scatter.1
